TPU v7x, 32 devices: a whole 2x2x4 slice. The times are simulated.
32 devices in a mesh: lists: 16 (over z, x, core), sub: 2 (over y).
Axes of the slice: x: 2, y: 2, z: 4, core: 2. Of those that a mesh axis runs over, the one named last changes fastest.
Arguments:
- vectors: bfloat16 [768, 6144], P('sub', 'lists'), may hold values from -6 to 6
- list_ids: int32 [6144], P('lists'), may hold values from 0 to 63
- counts: int32 [16, 16], replicated, may hold values from 0 to 24, as said below
- coarse: bfloat16 [768, 1024], P(None, ('lists', 'sub')), may hold values from -3 to 3
- codebook_init: float32 [768, 256], P('sub'), may hold values from -6 to 6
- codes: int32 [2, 96, 6144], P(None, 'sub', 'lists'), may hold values from 0 to 255
Outputs:
- codebook: float32 [768, 256], P('sub')
- leftover: bfloat16 [768, 6144], P('sub', 'lists')
Inputs may be any that keep to these rules, and one draw needn't show every extreme that they name: `counts`: counts of used slots in each block; in every draw one owner receives full blocks of 24 from every sender. `list_ids`: every slot names one of its block owner's lists.
All inputs are finite; a program needn't handle non-finite values.
Results may differ from a plain program's by a relative error of at most 0.0051.
Values may be sent and summed in bfloat16 or wider, within the bound.
A program may use at most 64 MiB of HBM per device.

v0:
```python
import jax
import jax.numpy as jnp
from jax import lax
from jax.sharding import PartitionSpec as P

K = 256
DS = 8
LISTS_DEV = 64
ITERS = 2


def shards(vectors, list_ids, counts, coarse, codebook_init, codes):
    features, rows = vectors.shape
    owners = lax.axis_size("lists")
    owner = lax.axis_index("lists")
    block = rows // owners
    subspaces = features // DS
    mine = lax.all_to_all(coarse, "sub", split_axis=0, concat_axis=1, tiled=True)
    list_iota = jnp.arange(LISTS_DEV, dtype=jnp.int32)
    arrived = lax.all_to_all(vectors, "lists", split_axis=1, concat_axis=1, tiled=True)
    labels = lax.all_to_all(
        list_ids.reshape(1, rows), "lists", split_axis=1, concat_axis=1, tiled=True
    ).reshape(rows)
    selector = (labels[None, :] == list_iota[:, None]).astype(jnp.bfloat16)
    centre = jnp.dot(mine, selector, preferred_element_type=jnp.float32)
    residual = (arrived.astype(jnp.float32) - centre).astype(jnp.bfloat16)
    block_counts = lax.dynamic_index_in_dim(counts, owner, 1, keepdims=False)
    valid = (jnp.arange(block, dtype=jnp.int32)[None, :] < block_counts[:, None]).reshape(rows)
    code_iota = jnp.arange(K, dtype=jnp.int32)
    split_res = residual.reshape(subspaces, DS, rows)
    group_size = 4
    groups = subspaces // group_size
    grouped_res = split_res.reshape(groups, group_size, DS, rows)
    grouped_codes = jnp.swapaxes(codes, 0, 1).reshape(groups, group_size, ITERS, rows)

    def group_sums(packed):
        sub_res, sub_codes = packed
        one_hot = (sub_codes[:, :, None, :] == code_iota[None, None, :, None]) & valid[
            None, None, None, :
        ]
        one_hot = one_hot.astype(jnp.bfloat16)
        sums = jnp.einsum("gdr,gtkr->tgdk", sub_res, one_hot, preferred_element_type=jnp.float32)
        tally = jnp.swapaxes(jnp.sum(one_hot, axis=3, dtype=jnp.float32), 0, 1)
        return (sums, tally)

    part_sums, part_counts = lax.map(group_sums, (grouped_res, grouped_codes))
    part_sums = jnp.swapaxes(part_sums, 0, 1).reshape(ITERS, features, K)
    part_counts = jnp.swapaxes(part_counts, 0, 1).reshape(ITERS, subspaces, K)
    weight = 0.25 * jnp.sum(counts).astype(jnp.float32) / K
    total_sums, total_counts = lax.psum((part_sums, part_counts), "lists")
    codebook = codebook_init
    for iteration in range(ITERS):
        spread = jnp.repeat(total_counts[iteration], DS, axis=0)
        codebook = (total_sums[iteration] + weight * codebook) / (spread + weight)
    high = codebook.astype(jnp.bfloat16)
    low = (codebook - high.astype(jnp.float32)).astype(jnp.bfloat16)
    books = jnp.concatenate(
        [high.reshape(subspaces, DS, K), low.reshape(subspaces, DS, K)], axis=1
    ).reshape(groups, group_size, 2 * DS, K)

    def group_pick(packed):
        book, sub_codes = packed
        one_hot = (sub_codes[:, None, :] == code_iota[None, :, None]).astype(jnp.bfloat16)
        both = jnp.einsum("gdk,gkr->gdr", book, one_hot, preferred_element_type=jnp.float32)
        return both[:, :DS] + both[:, DS:]

    picked = lax.map(group_pick, (books, grouped_codes[:, :, ITERS - 1]))
    picked = picked.reshape(subspaces, DS, rows)
    leftover = jnp.where(valid[None, None, :], split_res.astype(jnp.float32) - picked, 0.0)
    leftover = leftover.astype(jnp.bfloat16).reshape(features, rows)
    return (codebook, leftover)


def solution(mesh):
    return jax.shard_map(
        shards,
        mesh=mesh,
        in_specs=(
            P("sub", "lists"),
            P("lists"),
            P(),
            P(None, ("lists", "sub")),
            P("sub", None),
            P(None, "sub", "lists"),
        ),
        out_specs=(P("sub", None), P("sub", "lists")),
        check_vma=False,
    )
```

profile of v0, /device:TPU:0, one launch (start us, length us, event | category | flops | bytes accessed | tf_op | source)
XLA Modules:
  0.0 176.7 jit_solution(4619838477152994786)
XLA Ops:
  7.2 1.4 all_to_all.28
  8.6 7.4 %all-to-all-start.1 = ((s32[1,16,24]{2,0,1:T(1,128)}), s32[1,16,24]{2,0,1:T(1,128)S(1)}, u32[]{:S(2)}, u32[]{:S(2)}) async-start(s32[1,16,24]{2,0,1:T(1,128)} %all_to_all.28), calls=%async_computation.1 | async-start | bytes 16384 | tf_op jit(solution)/shard_map/all_to_all | solution.py:21
  16.0 1.9 %copy.21 = bf16[384,384]{0,1:T(8,128)(2,1)} copy(bf16[384,384]{1,0:T(8,128)(2,1)} %param.10) | data formatting | bytes 589824 | tf_op args[0]
  17.8 4.5 %all-to-all-done.1 = s32[1,16,24]{2,0,1:T(1,128)S(1)} async-done(((s32[1,16,24]{2,0,1:T(1,128)}), s32[1,16,24]{2,0,1:T(1,128)S(1)}, u32[]{:S(2)}, u32[]{:S(2)}) %all-to-all-start.1) | async-done | bytes 1568 | tf_op jit(solution)/shard_map/all_to_all | solution.py:21
  22.3 3.5 %all-to-all-start = ((bf16[384,16,24]{0,2,1:T(8,128)(2,1)}), bf16[384,16,24]{0,2,1:T(8,128)(2,1)S(1)}, u32[]{:S(2)}, u32[]{:S(2)}) async-start(bf16[384,16,24]{0,2,1:T(8,128)(2,1)} %bitcast.1), calls=%async_computation | async-start | bytes 589824 | tf_op jit(solution)/shard_map/all_to_all | solution.py:20
  29.4 7.0 %all-to-all-done = bf16[384,16,24]{0,2,1:T(8,128)(2,1)S(1)} async-done(((bf16[384,16,24]{0,2,1:T(8,128)(2,1)}), bf16[384,16,24]{0,2,1:T(8,128)(2,1)S(1)}, u32[]{:S(2)}, u32[]{:S(2)}) %all-to-all-start) | async-done | bytes 294944 | tf_op jit(solution)/shard_map/all_to_all | solution.py:20
  36.4 3.3 %all-to-all-start.2 = ((bf16[2,384,32]{1,2,0:T(8,128)(2,1)}), bf16[2,384,32]{1,2,0:T(8,128)(2,1)S(1)}, u32[]{:S(2)}, u32[]{:S(2)}) async-start(bf16[2,384,32]{1,2,0:T(8,128)(2,1)} %bitcast.93), calls=%async_computation.2 | async-start | bytes 98304 | tf_op jit(solution)/shard_map/all_to_all | solution.py:18
  40.0 3.7 %all-to-all-done.2 = bf16[2,384,32]{1,2,0:T(8,128)(2,1)S(1)} async-done(((bf16[2,384,32]{1,2,0:T(8,128)(2,1)}), bf16[2,384,32]{1,2,0:T(8,128)(2,1)S(1)}, u32[]{:S(2)}, u32[]{:S(2)}) %all-to-all-start.2) | async-done | bytes 49184 | tf_op jit(solution)/shard_map/all_to_all | solution.py:18
  44.0 25.4 %while.24 = (s32[]{:T(128)}, f32[12,2,4,8,256]{4,3,1,2,0:T(8,128)S(1)}, f32[12,2,4,256]{3,1,2,0:T(2,128)}, s32[12,4,2,384]{3,1,0,2:T(4,128)S(1)}, bf16[12,4,8,38...) while((s32[]{:T(128)}, f32[12,2,4,8,256]{4,3,1,2,0:T(8,128)S(1)}, ...), condition=%wide.region_2.3_spmd.clone, body=%wide.region_0.2_spmd.clone.sunk | while | flops 18086272 | bytes 192145 | solution.py:46
  44.2 0.7 fusion.48
  46.3 0.7 fusion.48
  48.4 0.7 fusion.48
  50.5 0.7 fusion.48
  52.6 0.7 fusion.48
  54.8 0.7 fusion.48
  56.9 0.7 fusion.48
  59.0 0.7 fusion.48
  61.1 0.7 fusion.48
  69.4 1.0 copy.25
  70.6 90.5 %all-reduce.3.cloned.1.call-done = (f32[2,384,256]{2,1,0:T(8,128)}, f32[2,48,256]{2,0,1:T(2,128)}) async-done(((f32[2,384,256]{2,1,0:T(8,128)}, f32[2,48,256]{2,0,1:T(2,128)}), (f32[2,384,256]{2,1,0:T(8,128)}, f32[2,48,256]{2,0,1:T(2,128)})) %all-reduce.3.cloned.1.call-update) | async-done | bytes 884752 | tf_op jit(solution)/shard_map/psum | solution.py:50
  161.1 1.1 slice_add_fusion.2
  162.2 2.0 %subtract_convert_fusion = (bf16[384,256]{1,0:T(8,128)(2,1)S(1)}, bf16[384,256]{1,0:T(8,128)(2,1)S(1)}, f32[384,256]{1,0:T(8,128)}) fusion(f32[48,256]{1,0:T(8,128)S(1)} %get-tuple-element.147, f32[48,256]{1,0:T(8,128)S(1)} %get-tuple-element.148, f32[384,256]{1,0:T(8,128)S(1)} %copy-done, f32[2,384,256]{2,1,0:T(8,128)} %get-tuple-element.140, f32[]{:T(128)S(6)} %div.9), kind=kLoop, calls=%fused_computation.43 | loop fusion | flops 983040 | bytes 2064388 | tf_op jit(solution)/shard_map/convert_element_type | solution.py:56
  164.2 4.8 %while.25 = (s32[]{:T(128)}, f32[12,4,8,384]{3,2,1,0:T(8,128)S(1)}, bf16[12,4,16,256]{3,2,1,0:T(8,128)(2,1)S(1)}, s32[12,4,384]{2,1,0:T(4,128)S(1)}, s32[]{:T(128)}) while((s32[]{:T(128)}, f32[12,4,8,384]{3,2,1,0:T(8,128)S(1)}, bf16[12,4,16,256]{3,2,1,0:T(8,128)(2,1)S(1)}, s32[12,4,384]{2,1,0:T(4,128)S(1)}, s32[]{:T(128)}) %tuple.52), condition=%wide.region_7.8_spmd.clone, body=%wide.region_6.7_spmd.clone.sunk | while | flops 12988418 | bytes 297033 | solution.py:67
  169.0 0.8 fusion.31
  (139 shorter events, 27.2 us)
Async XLA Ops:
  7.2 18.7 %copy-start.2 = (bf16[768,32]{0,1:T(8,128)(2,1)S(1)}, bf16[768,32]{0,1:T(8,128)(2,1)}, u32[]{:S(2)}) copy-start(bf16[768,32]{0,1:T(8,128)(2,1)} %param.13) | copy-start | bytes 147460
  7.2 19.3 %copy-start.1 = (s32[2,48,384]{2,1,0:T(8,128)S(1)}, s32[2,48,384]{2,1,0:T(8,128)}, u32[]{:S(2)}) copy-start(s32[2,48,384]{2,1,0:T(8,128)} %param.15) | copy-start | bytes 442372
  8.6 13.7 %all-to-all-start.1 = ((s32[1,16,24]{2,0,1:T(1,128)}), s32[1,16,24]{2,0,1:T(1,128)S(1)}, u32[]{:S(2)}, u32[]{:S(2)}) async-start(s32[1,16,24]{2,0,1:T(1,128)} %all_to_all.28), calls=%async_computation.1 | async-start | bytes 16384 | tf_op jit(solution)/shard_map/all_to_all | solution.py:21
  16.0 10.6 %copy-start.3 = (s32[16,16]{1,0:T(8,128)S(1)}, s32[16,16]{1,0:T(8,128)}, u32[]{:S(2)}) copy-start(s32[16,16]{1,0:T(8,128)} %param.12) | copy-start | bytes 3076
  22.3 14.1 %all-to-all-start = ((bf16[384,16,24]{0,2,1:T(8,128)(2,1)}), bf16[384,16,24]{0,2,1:T(8,128)(2,1)S(1)}, u32[]{:S(2)}, u32[]{:S(2)}) async-start(bf16[384,16,24]{0,2,1:T(8,128)(2,1)} %bitcast.1), calls=%async_computation | async-start | bytes 589824 | tf_op jit(solution)/shard_map/all_to_all | solution.py:20
  36.4 7.3 %all-to-all-start.2 = ((bf16[2,384,32]{1,2,0:T(8,128)(2,1)}), bf16[2,384,32]{1,2,0:T(8,128)(2,1)S(1)}, u32[]{:S(2)}, u32[]{:S(2)}) async-start(bf16[2,384,32]{1,2,0:T(8,128)(2,1)} %bitcast.93), calls=%async_computation.2 | async-start | bytes 98304 | tf_op jit(solution)/shard_map/all_to_all | solution.py:18
  39.7 121.4 %all-reduce.3.cloned.1.call-start = ((), (), s32[]{:S(2)}) async-start(), calls=%async_computation.3 | async-start | bytes 1769472 | tf_op jit(solution)/shard_map/psum | solution.py:50
  70.3 91.8 %copy-start = (f32[384,256]{1,0:T(8,128)S(1)}, f32[384,256]{1,0:T(8,128)}, u32[]{:S(2)}) copy-start(f32[384,256]{1,0:T(8,128)} %param.14) | copy-start | bytes 1179652
Sparse Core Ops, SparseCore 0:
  70.5 90.5 all-reduce.2
where the time goes:
time: 177 us
  waiting for transfers between devices  106 us (60%)
  local copies, waits for them, and re-layouts  14.8 us (8%)
  between operations  14.8 us (8%)
  starting transfers between devices  14.2 us (8%)
  other arithmetic  13.8 us (8%)
  matrix products  12.8 us (7%)
    psum x1, waiting for transfers between devices, shards(): total_sums, total_counts = lax.psum((part_sums, part_counts), 'lists')  90.5 us
    dot_general x12, matrix products, group_sums(): jnp.einsum('gdr,gtkr->tgdk', sub_res, one_hot, preferred_element_type=jnp...  8.24 us
    reduce_sum x12, other arithmetic, group_sums(): tally = jnp.swapaxes(jnp.sum(one_hot, axis=3, dtype=jnp.float32), 0, 1)  7.52 us
    all_to_all x1, starting transfers between devices, shards(): lax.all_to_all(list_ids.reshape(1, rows), 'lists', split_axis=1, concat_a...  7.36 us
    dynamic_update_slice x12, local copies, waits for them, and re-layouts, shards(): part_sums, part_counts = lax.map(group_sums, (grouped_res, grouped_codes))  7.27 us
    all_to_all x1, waiting for transfers between devices, shards(): lax.all_to_all(vectors, 'lists', split_axis=1, concat_axis=1, tiled=True)  7 us
    all_to_all x1, waiting for transfers between devices, shards(): lax.all_to_all(list_ids.reshape(1, rows), 'lists', split_axis=1, concat_a...  4.47 us
    dot_general x12, matrix products, group_pick(): jnp.einsum('gdk,gkr->gdr', book, one_hot, preferred_element_type=jnp.floa...  4.29 us
  transfers between devices with their start and end apart: 4, of which 4 were waited for; matrix products, arithmetic and copies ran while one was open for 3% of the time, Pallas kernels for 0%

commit v1 on v0

--- a/solution.py
+++ b/solution.py
@@ -9,6 +9,18 @@
 ITERS = 2
 
 
+def in_blocks(x, dim, devices):
+    shape = x.shape
+    pieces = x.reshape(*shape[:dim], devices, shape[dim] // devices, *shape[dim + 1 :])
+    return jnp.moveaxis(pieces, dim, 0)
+
+
+def in_order(pieces, dim):
+    pieces = jnp.moveaxis(pieces, 0, dim)
+    dims = pieces.shape
+    return pieces.reshape(*dims[:dim], dims[dim] * dims[dim + 1], *dims[dim + 2 :])
+
+
 def shards(vectors, list_ids, counts, coarse, codebook_init, codes):
     features, rows = vectors.shape
     owners = lax.axis_size("lists")
@@ -17,7 +29,15 @@
     subspaces = features // DS
     mine = lax.all_to_all(coarse, "sub", split_axis=0, concat_axis=1, tiled=True)
     list_iota = jnp.arange(LISTS_DEV, dtype=jnp.int32)
-    arrived = lax.all_to_all(vectors, "lists", split_axis=1, concat_axis=1, tiled=True)
+    count, index = (lax.axis_size("lists"), lax.axis_index("lists"))
+    pieces = in_blocks(vectors, 1, count)
+    out = pieces
+    for step in range(1, count):
+        target, source = ((index + step) % count, (index - step) % count)
+        sent = lax.dynamic_index_in_dim(pieces, target, 0)
+        received = lax.ppermute(sent, "lists", [(i, (i + step) % count) for i in range(count)])
+        out = lax.dynamic_update_slice_in_dim(out, received, source, axis=0)
+    arrived = in_order(out, 1)
     labels = lax.all_to_all(
         list_ids.reshape(1, rows), "lists", split_axis=1, concat_axis=1, tiled=True
     ).reshape(rows)

time: 177 us -> 187 us (1.056)
  starting transfers between devices: 14.2 us -> 30.4 us
  waiting for transfers between devices: 106 us -> 99.6 us
    ppermute x0 -> x15, starting transfers between devices: none -> 21.3 us  [shards(): lax.ppermute(sent, 'lists', [(i, (i + step) % count) for i in range(count)])]
    all_to_all x1 -> x0, waiting for transfers between devices: 7 us -> none  [shards(): lax.all_to_all(vectors, 'lists', split_axis=1, concat_axis=1, tiled=True)]
    psum x1, waiting for transfers between devices: 90.5 us -> 94.4 us  [shards(): total_sums, total_counts = lax.psum((part_sums, part_counts), 'lists')]
    all_to_all x1, waiting for transfers between devices: 3.66 us -> 0.01 us  [shards(): lax.all_to_all(coarse, 'sub', split_axis=0, concat_axis=1, tiled=True)]
    all_to_all x1 -> x0, starting transfers between devices: 3.54 us -> none  [shards(): lax.all_to_all(vectors, 'lists', split_axis=1, concat_axis=1, tiled=True)]
  transfers between devices with their start and end apart: 4 -> 18, of which waited for: 4 -> 4; matrix products, arithmetic and copies ran while one was open for 3% -> 2% of each run, Pallas kernels for 0% -> 0%
where the time goes in v1:
time: 187 us; the launch traced here: 186 us
  waiting for transfers between devices  99.6 us (53%)
  starting transfers between devices  30.4 us (16%)
  between operations  15.6 us (8%)
  other arithmetic  13.8 us (7%)
  local copies, waits for them, and re-layouts  13.7 us (7%)
  matrix products  12.8 us (7%)
    psum x1, waiting for transfers between devices, shards(): total_sums, total_counts = lax.psum((part_sums, part_counts), 'lists')  94.4 us
    ppermute x15, starting transfers between devices, shards(): lax.ppermute(sent, 'lists', [(i, (i + step) % count) for i in range(count)])  21.3 us
    dot_general x12, matrix products, group_sums(): jnp.einsum('gdr,gtkr->tgdk', sub_res, one_hot, preferred_element_type=jnp...  8.24 us
    reduce_sum x12, other arithmetic, group_sums(): tally = jnp.swapaxes(jnp.sum(one_hot, axis=3, dtype=jnp.float32), 0, 1)  7.52 us
    dynamic_update_slice x12, local copies, waits for them, and re-layouts, shards(): part_sums, part_counts = lax.map(group_sums, (grouped_res, grouped_codes))  7.27 us
    all_to_all x1, starting transfers between devices, shards(): lax.all_to_all(list_ids.reshape(1, rows), 'lists', split_axis=1, concat_a...  5.76 us
    dot_general x12, matrix products, group_pick(): jnp.einsum('gdk,gkr->gdr', book, one_hot, preferred_element_type=jnp.floa...  4.29 us
    all_to_all x1, waiting for transfers between devices, shards(): lax.all_to_all(list_ids.reshape(1, rows), 'lists', split_axis=1, concat_a...  3.8 us
  transfers between devices with their start and end apart: 18, of which 4 were waited for; matrix products, arithmetic and copies ran while one was open for 2% of the time, Pallas kernels for 0%

profile of v1, /device:TPU:0, one launch (start us, length us, event | category | flops | bytes accessed | tf_op | source)
XLA Modules:
  0.0 186.4 jit_solution(12549656879039960394)
XLA Ops:
  7.4 1.2 copy.21
  9.3 2.6 %collective-permute-start.1 = (bf16[1,384,24]{1,2,0:T(8,128)(2,1)S(1)}, bf16[1,384,24]{1,2,0:T(8,128)(2,1)S(1)}, u32[]{:S(2)}, u32[]{:S(2)}) collective-permute-start(bf16[1,384,24]{1,2,0:T(8,128)(2,1)S(1)} %get-tuple-element.158), channel_id=1, source_target_pairs={{0,4},{2,6},{4,8},{6,10},{8,12},{10,14},{12,16},{14,18},{16,20},{1... | collective-permute-start | bytes 55304 | tf_op jit(solution)/shard_map/ppermute | solution.py:38
  11.8 2.4 %collective-permute-start.2 = (bf16[1,384,24]{1,2,0:T(8,128)(2,1)S(1)}, bf16[1,384,24]{1,2,0:T(8,128)(2,1)S(1)}, u32[]{:S(2)}, u32[]{:S(2)}) collective-permute-start(bf16[1,384,24]{1,2,0:T(8,128)(2,1)S(1)} %get-tuple-element.157), channel_id=1, source_target_pairs={{0,6},{2,8},{4,10},{6,12},{8,14},{10,16},{12,18},{14,20},{16,22},{... | collective-permute-start | bytes 55304 | tf_op jit(solution)/shard_map/ppermute | solution.py:38
  14.2 1.6 collective-permute-start.3
  16.0 0.7 all_to_all.20
  16.7 5.8 %all-to-all-start = ((s32[1,16,24]{2,0,1:T(1,128)}), s32[1,16,24]{2,0,1:T(1,128)S(1)}, u32[]{:S(2)}, u32[]{:S(2)}) async-start(s32[1,16,24]{2,0,1:T(1,128)} %all_to_all.20), calls=%async_computation | async-start | bytes 16384 | tf_op jit(solution)/shard_map/all_to_all | solution.py:41
  25.1 3.8 %all-to-all-done = s32[1,16,24]{2,0,1:T(1,128)S(1)} async-done(((s32[1,16,24]{2,0,1:T(1,128)}), s32[1,16,24]{2,0,1:T(1,128)S(1)}, u32[]{:S(2)}, u32[]{:S(2)}) %all-to-all-start) | async-done | bytes 1568 | tf_op jit(solution)/shard_map/all_to_all | solution.py:41
  28.9 3.3 %all-to-all-start.1 = ((bf16[2,384,32]{1,2,0:T(8,128)(2,1)}), bf16[2,384,32]{1,2,0:T(8,128)(2,1)S(1)}, u32[]{:S(2)}, u32[]{:S(2)}) async-start(bf16[2,384,32]{1,2,0:T(8,128)(2,1)} %bitcast.121), calls=%async_computation.1 | async-start | bytes 98304 | tf_op jit(solution)/shard_map/all_to_all | solution.py:30
  34.0 0.7 collective-permute-start.6
  34.7 2.4 %collective-permute-start.7 = (bf16[1,384,24]{1,2,0:T(8,128)(2,1)S(1)}, bf16[1,384,24]{1,2,0:T(8,128)(2,1)S(1)}, u32[]{:S(2)}, u32[]{:S(2)}) collective-permute-start(bf16[1,384,24]{1,2,0:T(8,128)(2,1)S(1)} %get-tuple-element.152), channel_id=1, source_target_pairs={{0,16},{2,18},{4,20},{6,22},{8,24},{10,26},{12,28},{14,30},{16,0},... | collective-permute-start | bytes 55304 | tf_op jit(solution)/shard_map/ppermute | solution.py:38
  37.2 3.2 %collective-permute-start.9 = (bf16[1,384,24]{1,2,0:T(8,128)(2,1)S(1)}, bf16[1,384,24]{1,2,0:T(8,128)(2,1)S(1)}, u32[]{:S(2)}, u32[]{:S(2)}) collective-permute-start(bf16[1,384,24]{1,2,0:T(8,128)(2,1)S(1)} %get-tuple-element.150), channel_id=1, source_target_pairs={{0,20},{2,22},{4,24},{6,26},{8,28},{10,30},{12,0},{14,2},{16,4},{1... | collective-permute-start | bytes 55304 | tf_op jit(solution)/shard_map/ppermute | solution.py:38
  40.4 2.5 %collective-permute-start.10 = (bf16[1,384,24]{1,2,0:T(8,128)(2,1)S(1)}, bf16[1,384,24]{1,2,0:T(8,128)(2,1)S(1)}, u32[]{:S(2)}, u32[]{:S(2)}) collective-permute-start(bf16[1,384,24]{1,2,0:T(8,128)(2,1)S(1)} %get-tuple-element.149), channel_id=1, source_target_pairs={{0,22},{2,24},{4,26},{6,28},{8,30},{10,0},{12,2},{14,4},{16,6},{18... | collective-permute-start | bytes 55304 | tf_op jit(solution)/shard_map/ppermute | solution.py:38
  43.0 1.2 collective-permute-start.12
  44.3 1.5 collective-permute-start.13
  45.7 1.9 %collective-permute-start.14 = (bf16[1,384,24]{1,2,0:T(8,128)(2,1)S(1)}, bf16[1,384,24]{1,2,0:T(8,128)(2,1)S(1)}, u32[]{:S(2)}, u32[]{:S(2)}) collective-permute-start(bf16[1,384,24]{1,2,0:T(8,128)(2,1)S(1)} %get-tuple-element.145), channel_id=1, source_target_pairs={{0,30},{2,0},{4,2},{6,4},{8,6},{10,8},{12,10},{14,12},{16,14},{18,... | collective-permute-start | bytes 55304 | tf_op jit(solution)/shard_map/ppermute | solution.py:38
  48.1 1.0 collective-permute-done.14
  49.7 25.4 %while.24 = (s32[]{:T(128)}, f32[12,2,4,8,256]{4,3,1,2,0:T(8,128)S(1)}, f32[12,2,4,256]{3,1,2,0:T(2,128)}, s32[12,4,2,384]{3,1,0,2:T(4,128)S(1)}, bf16[12,4,8,38...) while((s32[]{:T(128)}, f32[12,2,4,8,256]{4,3,1,2,0:T(8,128)S(1)}, ...), condition=%wide.region_2.3_spmd.clone, body=%wide.region_0.2_spmd.clone.sunk | while | flops 18086272 | bytes 192145 | solution.py:66
  58.4 0.7 fusion.46
  75.1 1.0 copy.25
  76.3 94.4 %all-reduce.3.cloned.1.call-done = (f32[2,384,256]{2,1,0:T(8,128)}, f32[2,48,256]{2,0,1:T(2,128)}) async-done(((f32[2,384,256]{2,1,0:T(8,128)}, f32[2,48,256]{2,0,1:T(2,128)}), (f32[2,384,256]{2,1,0:T(8,128)}, f32[2,48,256]{2,0,1:T(2,128)})) %all-reduce.3.cloned.1.call-update) | async-done | bytes 884752 | tf_op jit(solution)/shard_map/psum | solution.py:70
  170.8 1.1 slice_add_fusion.2
  171.9 2.0 %subtract_convert_fusion.1 = (bf16[384,256]{1,0:T(8,128)(2,1)S(1)}, bf16[384,256]{1,0:T(8,128)(2,1)S(1)}, f32[384,256]{1,0:T(8,128)}) fusion(f32[48,256]{1,0:T(8,128)S(1)} %get-tuple-element.162, f32[48,256]{1,0:T(8,128)S(1)} %get-tuple-element.163, f32[384,256]{1,0:T(8,128)S(1)} %copy-done, f32[2,384,256]{2,1,0:T(8,128)} %get-tuple-element.140, f32[]{:T(128)S(6)} %div.9), kind=kLoop, calls=%fused_computation.42 | loop fusion | flops 983040 | bytes 2064388 | tf_op jit(solution)/shard_map/convert_element_type | solution.py:76
  173.9 4.8 %while.25 = (s32[]{:T(128)}, f32[12,4,8,384]{3,2,1,0:T(8,128)S(1)}, bf16[12,4,16,256]{3,2,1,0:T(8,128)(2,1)S(1)}, s32[12,4,384]{2,1,0:T(4,128)S(1)}, s32[]{:T(128)}) while((s32[]{:T(128)}, f32[12,4,8,384]{3,2,1,0:T(8,128)S(1)}, bf16[12,4,16,256]{3,2,1,0:T(8,128)(2,1)S(1)}, s32[12,4,384]{2,1,0:T(4,128)S(1)}, s32[]{:T(128)}) %tuple.66), condition=%wide.region_7.8_spmd.clone, body=%wide.region_6.7_spmd.clone.sunk | while | flops 12988418 | bytes 297033 | solution.py:87
  178.7 0.8 fusion.29
  (186 shorter events, 34.7 us)
Async XLA Ops:
  7.2 8.8 %copy-start.4 = (s32[384]{0:T(512)S(1)}, s32[384]{0:T(512)}, u32[]{:S(2)}) copy-start(s32[384]{0:T(512)} %param.11) | copy-start | bytes 4612
  7.4 15.4 %copy-start.2 = (bf16[768,32]{0,1:T(8,128)(2,1)S(1)}, bf16[768,32]{0,1:T(8,128)(2,1)}, u32[]{:S(2)}) copy-start(bf16[768,32]{0,1:T(8,128)(2,1)} %param.13) | copy-start | bytes 147460
  7.4 16.1 %copy-start.1 = (s32[2,48,384]{2,1,0:T(8,128)S(1)}, s32[2,48,384]{2,1,0:T(8,128)}, u32[]{:S(2)}) copy-start(s32[2,48,384]{2,1,0:T(8,128)} %param.15) | copy-start | bytes 442372
  8.6 14.9 %copy-start.3 = (s32[16,16]{1,0:T(8,128)S(1)}, s32[16,16]{1,0:T(8,128)}, u32[]{:S(2)}) copy-start(s32[16,16]{1,0:T(8,128)} %param.12) | copy-start | bytes 3076
  8.8 24.6 %collective-permute-start = (bf16[1,384,24]{1,2,0:T(8,128)(2,1)S(1)}, bf16[1,384,24]{1,2,0:T(8,128)(2,1)S(1)}, u32[]{:S(2)}, u32[]{:S(2)}) collective-permute-start(bf16[1,384,24]{1,2,0:T(8,128)(2,1)S(1)} %get-tuple-element.159), channel_id=1, source_target_pairs={{0,2},{2,4},{4,6},{6,8},{8,10},{10,12},{12,14},{14,16},{16,18},{18... | collective-permute-start | bytes 55304 | tf_op jit(solution)/shard_map/ppermute | solution.py:38
  9.3 24.7 %collective-permute-start.1 = (bf16[1,384,24]{1,2,0:T(8,128)(2,1)S(1)}, bf16[1,384,24]{1,2,0:T(8,128)(2,1)S(1)}, u32[]{:S(2)}, u32[]{:S(2)}) collective-permute-start(bf16[1,384,24]{1,2,0:T(8,128)(2,1)S(1)} %get-tuple-element.158), channel_id=1, source_target_pairs={{0,4},{2,6},{4,8},{6,10},{8,12},{10,14},{12,16},{14,18},{16,20},{1... | collective-permute-start | bytes 55304 | tf_op jit(solution)/shard_map/ppermute | solution.py:38
  11.8 22.9 %collective-permute-start.2 = (bf16[1,384,24]{1,2,0:T(8,128)(2,1)S(1)}, bf16[1,384,24]{1,2,0:T(8,128)(2,1)S(1)}, u32[]{:S(2)}, u32[]{:S(2)}) collective-permute-start(bf16[1,384,24]{1,2,0:T(8,128)(2,1)S(1)} %get-tuple-element.157), channel_id=1, source_target_pairs={{0,6},{2,8},{4,10},{6,12},{8,14},{10,16},{12,18},{14,20},{16,22},{... | collective-permute-start | bytes 55304 | tf_op jit(solution)/shard_map/ppermute | solution.py:38
  14.2 22.9 %collective-permute-start.3 = (bf16[1,384,24]{1,2,0:T(8,128)(2,1)S(1)}, bf16[1,384,24]{1,2,0:T(8,128)(2,1)S(1)}, u32[]{:S(2)}, u32[]{:S(2)}) collective-permute-start(bf16[1,384,24]{1,2,0:T(8,128)(2,1)S(1)} %get-tuple-element.156), channel_id=1, source_target_pairs={{0,8},{2,10},{4,12},{6,14},{8,16},{10,18},{12,20},{14,22},{16,24},... | collective-permute-start | bytes 55304 | tf_op jit(solution)/shard_map/ppermute | solution.py:38
  15.8 21.4 %collective-permute-start.4 = (bf16[1,384,24]{1,2,0:T(8,128)(2,1)S(1)}, bf16[1,384,24]{1,2,0:T(8,128)(2,1)S(1)}, u32[]{:S(2)}, u32[]{:S(2)}) collective-permute-start(bf16[1,384,24]{1,2,0:T(8,128)(2,1)S(1)} %get-tuple-element.155), channel_id=1, source_target_pairs={{0,10},{2,12},{4,14},{6,16},{8,18},{10,20},{12,22},{14,24},{16,26}... | collective-permute-start | bytes 55304 | tf_op jit(solution)/shard_map/ppermute | solution.py:38
  16.7 12.2 %all-to-all-start = ((s32[1,16,24]{2,0,1:T(1,128)}), s32[1,16,24]{2,0,1:T(1,128)S(1)}, u32[]{:S(2)}, u32[]{:S(2)}) async-start(s32[1,16,24]{2,0,1:T(1,128)} %all_to_all.20), calls=%async_computation | async-start | bytes 16384 | tf_op jit(solution)/shard_map/all_to_all | solution.py:41
  28.9 20.5 %all-to-all-start.1 = ((bf16[2,384,32]{1,2,0:T(8,128)(2,1)}), bf16[2,384,32]{1,2,0:T(8,128)(2,1)S(1)}, u32[]{:S(2)}, u32[]{:S(2)}) async-start(bf16[2,384,32]{1,2,0:T(8,128)(2,1)} %bitcast.121), calls=%async_computation.1 | async-start | bytes 98304 | tf_op jit(solution)/shard_map/all_to_all | solution.py:30
  32.1 138.6 %all-reduce.3.cloned.1.call-start = ((), (), s32[]{:S(2)}) async-start(), calls=%async_computation.2 | async-start | bytes 1769472 | tf_op jit(solution)/shard_map/psum | solution.py:70
  33.4 7.0 %collective-permute-start.5 = (bf16[1,384,24]{1,2,0:T(8,128)(2,1)S(1)}, bf16[1,384,24]{1,2,0:T(8,128)(2,1)S(1)}, u32[]{:S(2)}, u32[]{:S(2)}) collective-permute-start(bf16[1,384,24]{1,2,0:T(8,128)(2,1)S(1)} %get-tuple-element.154), channel_id=1, source_target_pairs={{0,12},{2,14},{4,16},{6,18},{8,20},{10,22},{12,24},{14,26},{16,28}... | collective-permute-start | bytes 55304 | tf_op jit(solution)/shard_map/ppermute | solution.py:38
  34.0 8.9 %collective-permute-start.6 = (bf16[1,384,24]{1,2,0:T(8,128)(2,1)S(1)}, bf16[1,384,24]{1,2,0:T(8,128)(2,1)S(1)}, u32[]{:S(2)}, u32[]{:S(2)}) collective-permute-start(bf16[1,384,24]{1,2,0:T(8,128)(2,1)S(1)} %get-tuple-element.153), channel_id=1, source_target_pairs={{0,14},{2,16},{4,18},{6,20},{8,22},{10,24},{12,26},{14,28},{16,30}... | collective-permute-start | bytes 55304 | tf_op jit(solution)/shard_map/ppermute | solution.py:38
  34.7 8.3 %collective-permute-start.7 = (bf16[1,384,24]{1,2,0:T(8,128)(2,1)S(1)}, bf16[1,384,24]{1,2,0:T(8,128)(2,1)S(1)}, u32[]{:S(2)}, u32[]{:S(2)}) collective-permute-start(bf16[1,384,24]{1,2,0:T(8,128)(2,1)S(1)} %get-tuple-element.152), channel_id=1, source_target_pairs={{0,16},{2,18},{4,20},{6,22},{8,24},{10,26},{12,28},{14,30},{16,0},... | collective-permute-start | bytes 55304 | tf_op jit(solution)/shard_map/ppermute | solution.py:38
  37.1 7.1 %collective-permute-start.8 = (bf16[1,384,24]{1,2,0:T(8,128)(2,1)S(1)}, bf16[1,384,24]{1,2,0:T(8,128)(2,1)S(1)}, u32[]{:S(2)}, u32[]{:S(2)}) collective-permute-start(bf16[1,384,24]{1,2,0:T(8,128)(2,1)S(1)} %get-tuple-element.151), channel_id=1, source_target_pairs={{0,18},{2,20},{4,22},{6,24},{8,26},{10,28},{12,30},{14,0},{16,2},{... | collective-permute-start | bytes 55304 | tf_op jit(solution)/shard_map/ppermute | solution.py:38
  37.2 8.5 %collective-permute-start.9 = (bf16[1,384,24]{1,2,0:T(8,128)(2,1)S(1)}, bf16[1,384,24]{1,2,0:T(8,128)(2,1)S(1)}, u32[]{:S(2)}, u32[]{:S(2)}) collective-permute-start(bf16[1,384,24]{1,2,0:T(8,128)(2,1)S(1)} %get-tuple-element.150), channel_id=1, source_target_pairs={{0,20},{2,22},{4,24},{6,26},{8,28},{10,30},{12,0},{14,2},{16,4},{1... | collective-permute-start | bytes 55304 | tf_op jit(solution)/shard_map/ppermute | solution.py:38
  40.4 7.2 %collective-permute-start.10 = (bf16[1,384,24]{1,2,0:T(8,128)(2,1)S(1)}, bf16[1,384,24]{1,2,0:T(8,128)(2,1)S(1)}, u32[]{:S(2)}, u32[]{:S(2)}) collective-permute-start(bf16[1,384,24]{1,2,0:T(8,128)(2,1)S(1)} %get-tuple-element.149), channel_id=1, source_target_pairs={{0,22},{2,24},{4,26},{6,28},{8,30},{10,0},{12,2},{14,4},{16,6},{18... | collective-permute-start | bytes 55304 | tf_op jit(solution)/shard_map/ppermute | solution.py:38
  42.9 4.7 %collective-permute-start.11 = (bf16[1,384,24]{1,2,0:T(8,128)(2,1)S(1)}, bf16[1,384,24]{1,2,0:T(8,128)(2,1)S(1)}, u32[]{:S(2)}, u32[]{:S(2)}) collective-permute-start(bf16[1,384,24]{1,2,0:T(8,128)(2,1)S(1)} %get-tuple-element.148), channel_id=1, source_target_pairs={{0,24},{2,26},{4,28},{6,30},{8,0},{10,2},{12,4},{14,6},{16,8},{18,... | collective-permute-start | bytes 55304 | tf_op jit(solution)/shard_map/ppermute | solution.py:38
  43.0 4.6 %collective-permute-start.12 = (bf16[1,384,24]{1,2,0:T(8,128)(2,1)S(1)}, bf16[1,384,24]{1,2,0:T(8,128)(2,1)S(1)}, u32[]{:S(2)}, u32[]{:S(2)}) collective-permute-start(bf16[1,384,24]{1,2,0:T(8,128)(2,1)S(1)} %get-tuple-element.147), channel_id=1, source_target_pairs={{0,26},{2,28},{4,30},{6,0},{8,2},{10,4},{12,6},{14,8},{16,10},{18,... | collective-permute-start | bytes 55304 | tf_op jit(solution)/shard_map/ppermute | solution.py:38
  44.3 3.8 %collective-permute-start.13 = (bf16[1,384,24]{1,2,0:T(8,128)(2,1)S(1)}, bf16[1,384,24]{1,2,0:T(8,128)(2,1)S(1)}, u32[]{:S(2)}, u32[]{:S(2)}) collective-permute-start(bf16[1,384,24]{1,2,0:T(8,128)(2,1)S(1)} %get-tuple-element.146), channel_id=1, source_target_pairs={{0,28},{2,30},{4,0},{6,2},{8,4},{10,6},{12,8},{14,10},{16,12},{18,... | collective-permute-start | bytes 55304 | tf_op jit(solution)/shard_map/ppermute | solution.py:38
  45.7 3.3 %collective-permute-start.14 = (bf16[1,384,24]{1,2,0:T(8,128)(2,1)S(1)}, bf16[1,384,24]{1,2,0:T(8,128)(2,1)S(1)}, u32[]{:S(2)}, u32[]{:S(2)}) collective-permute-start(bf16[1,384,24]{1,2,0:T(8,128)(2,1)S(1)} %get-tuple-element.145), channel_id=1, source_target_pairs={{0,30},{2,0},{4,2},{6,4},{8,6},{10,8},{12,10},{14,12},{16,14},{18,... | collective-permute-start | bytes 55304 | tf_op jit(solution)/shard_map/ppermute | solution.py:38
  76.1 95.7 %copy-start = (f32[384,256]{1,0:T(8,128)S(1)}, f32[384,256]{1,0:T(8,128)}, u32[]{:S(2)}) copy-start(f32[384,256]{1,0:T(8,128)} %param.14) | copy-start | bytes 1179652
Sparse Core Ops, SparseCore 0:
  76.3 94.4 all-reduce.2
